TPU v7x, 32 devices: a whole 2x2x4 slice. The times are simulated.
32 devices in a mesh: grp: 2 (over y), row: 8 (over z, x), blk: 2 (over core).
Axes of the slice: x: 2, y: 2, z: 4, core: 2. Of those that a mesh axis runs over, the one named last changes fastest.
Arguments:
- density: float32 [64, 5, 128, 128], P(('grp', 'row'), None, 'blk'), parts along dimension 0, may hold values from -1 to 2, as said below
- pattern: int32 [64, 5], P(('grp', 'row')), parts along dimension 0, may hold values from 0 to 1, as said below
Outputs:
- purified: float32 [64, 5, 128, 128], P(('grp', 'row'), None, 'blk'), parts along dimension 0
- occupancy: float32 [4], P('grp'), parts along dimension 0
There are 2 independent parts, one for each index of `grp`. A program takes and returns all parts, laid end to end along the dimension named above; each array names one. Nothing has to cross between parts.
Inputs may be any that keep to these rules, and one draw needn't show every extreme that they name: pattern[i, 2] = 1 and pattern[i, 2 + o] = pattern[(i + o) mod 32, 2 - o]. `density`: zero in every block whose pattern entry is 0; block (i, 2 + o) is the transpose of block ((i + o) mod 32, 2 - o).
All inputs are finite; a program needn't handle non-finite values.
Results may differ from a plain program's by a relative error of at most 0.00016.
Values sent between devices are 32-bit elements; how exact they have to be, the bound alone decides.
A program may use at most 64 MiB of HBM per device.

v0:
```python
import jax
import jax.numpy as jnp
from jax import lax
from jax.sharding import PartitionSpec as P

W = 2
ITERS = 2


def padded(shard, sides, width):
    for axis, dim in sides:
        size, length = (lax.axis_size(axis), shard.shape[dim])
        up = [(i, (i + 1) % size) for i in range(size)]
        down = [(j, i) for i, j in up]
        last = lax.slice_in_dim(shard, length - width, length, axis=dim)
        first = lax.slice_in_dim(shard, 0, width, axis=dim)
        before = lax.ppermute(last, axis, up)
        after = lax.ppermute(first, axis, down)
        shard = jnp.concatenate([before, shard, after], axis=dim)
    return shard


def block_product(left, right, pattern):
    rows = left.shape[0]
    blocks = []
    for out_off in range(-W, W + 1):
        total = jnp.zeros((rows, left.shape[2], right.shape[3]), jnp.float32)
        for term in range(-W, W + 1):
            other = out_off - term
            if abs(other) > W:
                continue
            total = total + jnp.einsum(
                "nxy,nyz->nxz",
                left[:, W + term],
                right[W + term : W + term + rows, W + other],
                precision=lax.Precision.HIGHEST,
            )
        blocks.append(total * pattern[:, W + out_off].astype(jnp.float32)[:, None, None])
    return jnp.stack(blocks, axis=1)


def step_total(partial_value):
    return lax.psum(partial_value, ("row", "blk"))


def local(density, pattern):
    own_rows = density.shape[0]
    order = jnp.float32(own_rows * lax.axis_size("row") * density.shape[3])
    partials = []
    occupancy = []
    half_rows = own_rows // 2
    whole_rows = lax.all_to_all(density, "blk", split_axis=0, concat_axis=2, tiled=True)
    row_mask = lax.dynamic_slice_in_dim(pattern, lax.axis_index("blk") * half_rows, half_rows, 0)
    for step in range(ITERS):
        extended = padded(whole_rows, ((("row", "blk"), 0),), W)
        square = block_product(whole_rows, extended, row_mask)
        cube = block_product(square, extended, row_mask)
        whole_rows = 3.0 * square - 2.0 * cube
        partials.append(jnp.einsum("nii->", whole_rows[:, W]) / order)
        occupancy.append(step_total(partials[-1]))
    current = lax.all_to_all(whole_rows, "blk", split_axis=2, concat_axis=0, tiled=True)
    totals = jnp.stack(occupancy)
    return (current, totals)


def solution(mesh):
    placed = (P(("grp", "row"), None, "blk", None), P(("grp", "row"), None))
    return jax.shard_map(
        local,
        mesh=mesh,
        in_specs=placed,
        out_specs=(P(("grp", "row"), None, "blk", None), P("grp")),
        check_vma=False,
    )
```

profile of v0, /device:TPU:0, one launch (start us, length us, event | category | flops | bytes accessed | tf_op | source)
XLA Modules:
  0.0 105.8 jit_solution(17886259436273899301)
XLA Ops:
  0.6 5.3 %all_to_all.36 = f32[4,5,64,128]{3,2,1,0:T(8,128)S(1)} all-to-all(f32[4,5,64,128]{3,2,1,0:T(8,128)} %param.2), channel_id=1, replica_groups=mesh['grp'=2,'row'=8,'blk'=2] {'blk'}, dimensions={0} | all-to-all | bytes 1310720 | tf_op jit(solution)/shard_map/all_to_all | solution.py:52
  6.2 5.6 %collective-permute-start.1 = (f32[2,5,128,128]{3,2,0,1:T(8,128)S(1)}, f32[2,5,128,128]{3,2,0,1:T(8,128)S(1)}, u32[]{:S(2)}, u32[]{:S(2)}) collective-permute-start(f32[2,5,128,128]{3,2,0,1:T(8,128)S(1)} %bitcast.368), channel_id=1, source_target_pairs={{1,0},{2,1},{3,2},{4,3},{5,4},{6,5},{7,6},{8,7},{9,8},{10,9},{11,1... | collective-permute-start | bytes 1966088 | tf_op jit(solution)/shard_map/ppermute | solution.py:18
  13.5 6.7 %collective-permute-done = f32[2,5,128,128]{3,2,0,1:T(8,128)S(1)} collective-permute-done((f32[2,5,128,128]{3,2,0,1:T(8,128)S(1)}, f32[2,5,128,128]{3,2,0,1:T(8,128)S(1)}, u32[]{:S(2)}, u32[]{:S(2)}) %collective-permute-start) | collective-permute-done | bytes 655392 | tf_op jit(solution)/shard_map/ppermute | solution.py:17
  21.4 0.3 bitcast_dynamic-update-slice_fusion.9
  22.5 0.3 bitcast_dynamic-update-slice_fusion.7
  25.5 0.3 bitcast_dynamic-update-slice_fusion.6
  26.4 0.3 fusion.60
  27.5 0.3 bitcast_dynamic-update-slice_fusion.5
  28.9 0.3 fusion.51
  29.5 6.0 %collective-permute-start.2 = (f32[2,5,128,128]{3,2,0,1:T(8,128)S(1)}, f32[2,5,128,128]{3,2,0,1:T(8,128)S(1)}, u32[]{:S(2)}, u32[]{:S(2)}) collective-permute-start(f32[2,5,128,128]{3,2,0,1:T(8,128)S(1)} %multiply_subtract_fusion.1), channel_id=1, source_target_pairs={{0,1},{1,2},{2,3},{3,4},{4,5},{5,6},{6,7},{7,8},{8,9},{9,10},{10,1... | collective-permute-start | bytes 1966088 | tf_op jit(solution)/shard_map/ppermute | solution.py:17
  36.9 5.5 %collective-permute-done.2 = f32[2,5,128,128]{3,2,0,1:T(8,128)S(1)} collective-permute-done((f32[2,5,128,128]{3,2,0,1:T(8,128)S(1)}, f32[2,5,128,128]{3,2,0,1:T(8,128)S(1)}, u32[]{:S(2)}, u32[]{:S(2)}) %collective-permute-start.2) | collective-permute-done | bytes 655392 | tf_op jit(solution)/shard_map/ppermute | solution.py:17
  42.4 1.2 %collective-permute-done.3 = f32[2,5,128,128]{3,2,0,1:T(8,128)S(1)} collective-permute-done((f32[2,5,128,128]{3,2,0,1:T(8,128)S(1)}, f32[2,5,128,128]{3,2,0,1:T(8,128)S(1)}, u32[]{:S(2)}, u32[]{:S(2)}) %collective-permute-start.3) | collective-permute-done | bytes 655392 | tf_op jit(solution)/shard_map/ppermute | solution.py:18
  44.9 0.3 bitcast_dynamic-update-slice_fusion.4
  46.0 0.3 bitcast_dynamic-update-slice_fusion.2
  49.0 0.3 bitcast_dynamic-update-slice_fusion.1
  50.4 0.3 fusion.32
  52.3 0.3 fusion.19
  53.0 0.5 copy.58
  53.5 0.6 select_reduce_fusion
  54.1 0.6 select_reduce_fusion.1
  56.1 10.2 %all_to_all.37 = f32[2,5,128,128]{3,0,1,2:T(2,128)S(1)} all-to-all(f32[2,5,128,128]{3,0,1,2:T(2,128)S(1)} %copy.58), channel_id=1, replica_groups=mesh['grp'=2,'row'=8,'blk'=2] {'blk'}, dimensions={2} | all-to-all | bytes 1310720 | tf_op jit(solution)/shard_map/all_to_all | solution.py:61
  66.3 0.9 copy.59
  67.2 36.8 %all-reduce = (f32[1]{0:T(128)}, f32[1]{0:T(128)}) all-reduce(f32[1]{0:T(128)} %bitcast.74, f32[1]{0:T(128)} %bitcast.73), channel_id=1, replica_groups=mesh['grp'=2,'row'=8,'blk'=2] {'row','blk'}, use_global_device_ids=true, to_apply=%region_5.0 | all-reduce | flops 2 | bytes 16 | tf_op jit(solution)/shard_map/psum | solution.py:43
  104.0 1.8 %pad_maximum_fusion.4 = f32[2]{0:T(128)} fusion(f32[1]{0:T(128)} %get-tuple-element.7, f32[1]{0:T(128)} %get-tuple-element.8), kind=kLoop, calls=%fused_computation.212 | loop fusion | flops 2 | bytes 16 | tf_op jit(solution)/shard_map/stack | solution.py:62
  (78 shorter events, 18.3 us)
Async XLA Ops:
  0.6 11.8 %copy-start = (s32[4,5]{1,0:T(4,128)S(1)}, s32[4,5]{1,0:T(4,128)}, u32[]{:S(2)}) copy-start(s32[4,5]{1,0:T(4,128)} %param.3) | copy-start | bytes 244
  6.0 14.1 %collective-permute-start = (f32[2,5,128,128]{3,2,0,1:T(8,128)S(1)}, f32[2,5,128,128]{3,2,0,1:T(8,128)S(1)}, u32[]{:S(2)}, u32[]{:S(2)}) collective-permute-start(f32[2,5,128,128]{3,2,0,1:T(8,128)S(1)} %bitcast.367), channel_id=1, source_target_pairs={{0,1},{1,2},{2,3},{3,4},{4,5},{5,6},{6,7},{7,8},{8,9},{9,10},{10,1... | collective-permute-start | bytes 1966088 | tf_op jit(solution)/shard_map/ppermute | solution.py:17
  6.2 14.0 %collective-permute-start.1 = (f32[2,5,128,128]{3,2,0,1:T(8,128)S(1)}, f32[2,5,128,128]{3,2,0,1:T(8,128)S(1)}, u32[]{:S(2)}, u32[]{:S(2)}) collective-permute-start(f32[2,5,128,128]{3,2,0,1:T(8,128)S(1)} %bitcast.368), channel_id=1, source_target_pairs={{1,0},{2,1},{3,2},{4,3},{5,4},{6,5},{7,6},{8,7},{9,8},{10,9},{11,1... | collective-permute-start | bytes 1966088 | tf_op jit(solution)/shard_map/ppermute | solution.py:18
  29.5 12.9 %collective-permute-start.2 = (f32[2,5,128,128]{3,2,0,1:T(8,128)S(1)}, f32[2,5,128,128]{3,2,0,1:T(8,128)S(1)}, u32[]{:S(2)}, u32[]{:S(2)}) collective-permute-start(f32[2,5,128,128]{3,2,0,1:T(8,128)S(1)} %multiply_subtract_fusion.1), channel_id=1, source_target_pairs={{0,1},{1,2},{2,3},{3,4},{4,5},{5,6},{6,7},{7,8},{8,9},{9,10},{10,1... | collective-permute-start | bytes 1966088 | tf_op jit(solution)/shard_map/ppermute | solution.py:17
  35.6 8.1 %collective-permute-start.3 = (f32[2,5,128,128]{3,2,0,1:T(8,128)S(1)}, f32[2,5,128,128]{3,2,0,1:T(8,128)S(1)}, u32[]{:S(2)}, u32[]{:S(2)}) collective-permute-start(f32[2,5,128,128]{3,2,0,1:T(8,128)S(1)} %multiply_subtract_fusion.1), channel_id=1, source_target_pairs={{1,0},{2,1},{3,2},{4,3},{5,4},{6,5},{7,6},{8,7},{9,8},{10,9},{11,1... | collective-permute-start | bytes 1966088 | tf_op jit(solution)/shard_map/ppermute | solution.py:18
where the time goes:
time: 106 us
  blocking collectives  52.4 us (49%)
  matrix products  20.4 us (19%)
  waiting for transfers between devices  13.4 us (13%)
  starting transfers between devices  11.9 us (11%)
  other arithmetic  3.61 us (3%)
  between operations  2.61 us (2%)
  local copies, waits for them, and re-layouts  1.49 us (1%)
    psum x1, blocking collectives, step_total(): return lax.psum(partial_value, ('row', 'blk'))  36.8 us
    dot_general x76, matrix products, block_product(): jnp.einsum('nxy,nyz->nxz', left[:, W + term], right[W + term:W + term + r...  20.4 us
    ppermute x2, waiting for transfers between devices, padded(): before = lax.ppermute(last, axis, up)  12.2 us
    all_to_all x1, blocking collectives, local(): lax.all_to_all(whole_rows, 'blk', split_axis=2, concat_axis=0, tiled=True)  10.2 us
    ppermute x2, starting transfers between devices, padded(): before = lax.ppermute(last, axis, up)  6.22 us
    ppermute x2, starting transfers between devices, padded(): after = lax.ppermute(first, axis, down)  5.65 us
    all_to_all x1, blocking collectives, local(): lax.all_to_all(density, 'blk', split_axis=0, concat_axis=2, tiled=True)  5.34 us
  transfers between devices with their start and end apart: 4, of which 3 were waited for; matrix products, arithmetic and copies ran while one was open for 3% of the time, Pallas kernels for 0%

commit v1 on v0

v1 whole, which is shorter than its diff:
```python
import functools

import jax
import jax.numpy as jnp
from jax import lax
from jax.experimental import pallas as pl
from jax.experimental.pallas import tpu as pltpu
from jax.sharding import PartitionSpec as P

MESH = pl.DeviceIdType.MESH
F32 = jnp.float32
BF16 = jnp.bfloat16

B = 128
G, H, M, N = range(4)


def span(first, last):
    return slice(first * 2 * B, (last + 1) * 2 * B)


def block(index):
    return slice(index * B, (index + 1) * B)


def store_split(high, low, at, value):
    top = value.astype(BF16)
    high[at] = top
    low[at] = (value - top.astype(F32)).astype(BF16)


def product(left, right, row, col, first, last):
    (lh, ll), (rh, rl) = left, right
    lat, rat = (span(row, row), span(first, last)), (span(first, last), span(col, col))
    dot = functools.partial(jnp.dot, preferred_element_type=F32)
    return dot(lh[lat], rh[rat]) + dot(lh[lat], rl[rat]) + dot(ll[lat], rh[rat])


def kernel(rows, dens, pat, out, occ, own, halo, dh, dl, sh, sl, s32, eh, el, xs, xr, res, patf, pathalo, tsend, trecv,
           own_send, own_recv, own_loc, halo_send, halo_recv, pat_sem, x_send, x_recv, t_sem, out_sem):
    r, b = lax.axis_index("row"), lax.axis_index("blk")
    devices = 2 * rows
    me = 2 * r + b
    sign = 1 - 2 * b
    half = pl.ds(pl.multiple_of(64 * b, 64), 64)
    other_half = pl.ds(pl.multiple_of(64 * (1 - b), 64), 64)
    after, before = lax.rem(r + 1, rows), lax.rem(r + rows - 1, rows)
    order = F32(4 * rows * B)

    def partner(j):
        p = lax.rem(me + j, devices)
        return {"row": p // 2, "blk": lax.rem(p, 2)}

    barrier = pltpu.get_barrier_semaphore()

    def greet(j, carry):
        pl.semaphore_signal(barrier, inc=1, device_id=partner(j), device_id_type=MESH)
        return carry

    lax.fori_loop(1, devices, greet, 0)
    local = []
    for i in range(4):
        copy = pltpu.make_async_copy(dens.at[i], own.at[i, :, half], own_loc.at[i])
        copy.start()
        local.append(copy)
    patf[...] = jnp.zeros_like(patf)
    patf[0:4, 0:5] = pat[...].astype(F32)
    pl.semaphore_wait(barrier, devices - 1)

    sends = []

    def send(src, dst, send_sem, recv_sem, device):
        copy = pltpu.make_async_remote_copy(src, dst, send_sem, recv_sem, device_id=device, device_id_type=MESH)
        copy.start()
        sends.append(copy)
        return copy

    def send_halo(d):
        n = min(3, 4 - d)
        send(dens.at[d, 2:2 + n], halo.at[d, 2:2 + n, half], halo_send.at[0, d], halo_recv.at[d, b],
             {"row": after, "blk": 0})
        send(dens.at[3 - d, 3 - n:3], halo.at[d, 3 - n:3, half], halo_send.at[1, d], halo_recv.at[d, b],
             {"row": before, "blk": 1})

    pats = send(patf, pathalo, pat_sem.at[0], pat_sem.at[1], {"row": jnp.where(b == 0, after, before), "blk": b})
    send_halo(3)
    send_halo(2)
    theirs = {}
    for q in range(4):
        i = 2 * (1 - b) + q if q < 2 else 2 * b + q - 2
        send(dens.at[i], own.at[i, :, half], own_send.at[q], own_recv.at[i], {"row": r, "blk": 1 - b})
    send_halo(1)
    send_halo(0)

    def wait_own(i):
        pltpu.make_async_copy(dens.at[i], own.at[i, :, half], own_loc.at[i]).wait()
        pltpu.make_async_remote_copy(dens.at[i], own.at[i, :, other_half], own_send.at[0], own_recv.at[i],
                                     device_id={"row": r, "blk": 1 - b}, device_id_type=MESH).wait_recv()

    def wait_halo(d):
        n = min(3, 4 - d)
        start = jnp.where(b == 0, 2, 3 - n)
        for c in range(2):
            at = halo.at[d, pl.ds(start, n), 64 * c:64 * c + 64]
            pltpu.make_async_remote_copy(at, at, halo_send.at[0, d], halo_recv.at[d, c],
                                         device_id={"row": r, "blk": 1 - b}, device_id_type=MESH).wait_recv()

    def own_row(d):
        return jnp.where(b == 0, d - 4, 7 - d)

    D, S, E = (dh, dl), (sh, sl), (eh, el)

    def put(d, e, value):
        store_split(dh, dl, (block(d), block(e)), value)

    def clear(pair, d, e):
        for ref in pair:
            ref[block(d), block(e)] = jnp.zeros((B, B), BF16)

    def mask(d, e):
        ref, i = (pathalo, jnp.where(b == 0, d, 3 - d)) if d < 4 else (patf, own_row(d))
        k = e - d + 2
        return jnp.where(b == 0, ref[pl.ds(i, 1), k:k + 1], ref[pl.ds(i, 1), 4 - k:5 - k])

    def blocks(I, J):
        for a in range(2):
            for c in range(2):
                yield a, c, 2 * I + a, 2 * J + c

    def square(source, I, J, first, last):
        total = product(source, source, I, J, first, last)
        for a, c, d, e in blocks(I, J):
            if abs(d - e) > 2:
                clear(S, d, e)
            else:
                value = total[block(a), block(c)] * mask(d, e)
                s32[block(d), block(e)] = value
                store_split(sh, sl, (block(d), block(e)), value)

    def update(source, I, J, first, last):
        total = product(S, source, I, J, first, last)
        for a, c, d, e in blocks(I, J):
            if abs(d - e) <= 2:
                yield d, e, 3.0 * s32[block(d), block(e)] - 2.0 * (total[block(a), block(c)] * mask(d, e))

    def keep(I, J, first, last):
        for d, e, value in update(D, I, J, first, last):
            store_split(eh, el, (block(d), block(e)), value)
            if d >= 4 and e >= 4:
                xs[e - 4, d - 4] = value
        for a, c, d, e in blocks(I, J):
            if abs(d - e) > 2:
                clear(E, d, e)

    eye = (lax.broadcasted_iota(jnp.int32, (B, B), 0) == lax.broadcasted_iota(jnp.int32, (B, B), 1)).astype(F32)

    def trace(first, second):
        return jnp.sum((first + second) * eye, axis=0, keepdims=True) / order

    for i in range(4):
        wait_own(i)
    for d in range(4, 8):
        for e in range(max(2, d - 2), min(8, d + 3)):
            value = own[own_row(d), 2 + sign * (e - d)]
            put(d, e, value)
            if e < 4:
                put(e, d, value.T)
    for d, e in ((2, 5), (5, 2), (4, 7), (7, 4)):
        clear(D, d, e)
    square(D, M, M, H, N)
    square(D, M, N, M, N)
    keep(M, N, M, N)
    xs[3, 0] = jnp.zeros((B, B), F32)
    other = {"row": r, "blk": 1 - b}
    send(xs.at[2:4], xr.at[2:4], x_send.at[0], x_recv.at[0], other)

    def put_halo(d):
        for k in range(min(3, 4 - d)):
            value = halo[d, 2 + sign * k]
            put(d, d + k, value)
            if k:
                put(d + k, d, value.T)

    wait_halo(3)
    put_halo(3)
    wait_halo(2)
    put_halo(2)
    square(D, M, H, H, M)
    keep(M, M, H, N)
    send(xs.at[0:2], xr.at[0:2], x_send.at[1], x_recv.at[1], other)
    tsend[...] = jnp.zeros_like(tsend)
    tsend[0:1, :] = trace(xs[0, 0], xs[1, 1])
    keep(M, H, H, M)
    pats.wait_recv()
    square(D, H, M, H, M)

    wait_halo(1)
    put_halo(1)
    wait_halo(0)
    put_halo(0)
    clear(D, 0, 3)
    clear(D, 3, 0)
    square(D, H, G, G, H)
    square(D, H, H, G, M)
    keep(H, H, G, M)
    keep(H, M, H, M)

    for part, at in ((0, slice(2, 4)), (1, slice(0, 2))):
        pltpu.make_async_remote_copy(xs.at[at], xr.at[at], x_send.at[part], x_recv.at[part], device_id=other,
                                     device_id_type=MESH).wait_recv()
    for a in range(2):
        for c in range(4):
            store_split(eh, el, (block(6 + a), block(4 + c)), xr[3 - c, 1 - a])
    square(E, M, M, H, N)
    square(E, M, H, H, M)
    square(E, M, N, M, N)

    def finish(J, first, last):
        kept = []
        for d, e, value in update(E, M, J, first, last):
            res[jnp.where(b == 0, d - 4, 5 - d), 2 + sign * (e - d)] = value
            if d == e:
                kept.append(value)
        return kept

    tsend[1:2, :] = trace(*finish(M, H, N))

    def tell(j, carry):
        pltpu.make_async_remote_copy(tsend, trecv.at[me], t_sem.at[0], t_sem.at[1], device_id=partner(j),
                                     device_id_type=MESH).start()
        return carry

    lax.fori_loop(1, devices, tell, 0)
    finish(H, H, M)
    finish(N, M, N)
    mine = pltpu.make_async_copy(res.at[:, :, half], out.at[pl.ds(2 * b, 2)], out_sem.at[0])
    mine.start()
    yours = pltpu.make_async_remote_copy(res.at[:, :, other_half], out.at[pl.ds(2 * b, 2)], out_sem.at[1],
                                         out_sem.at[2], device_id=other, device_id_type=MESH)
    yours.start()
    all_but_one = trecv.at[0:devices - 1]
    told = pltpu.make_async_remote_copy(all_but_one, all_but_one, t_sem.at[0], t_sem.at[1], device_id=other,
                                        device_id_type=MESH)
    told.wait_recv()
    trecv[me] = tsend[...]
    total = jnp.sum(trecv[...], axis=0)
    occ[0] = jnp.sum(total[0:1, :])
    occ[1] = jnp.sum(total[1:2, :])
    told.wait_send()
    for copy in sends:
        copy.wait_send()
    mine.wait()
    yours.wait()


def local(density, pattern):
    rows = lax.axis_size("row")
    dma = pltpu.SemaphoreType.DMA
    wide = 8 * B
    return pl.pallas_call(
        functools.partial(kernel, rows),
        out_shape=(jax.ShapeDtypeStruct(density.shape, F32), jax.ShapeDtypeStruct((2,), F32)),
        in_specs=[pl.BlockSpec(memory_space=pl.ANY), pl.BlockSpec(memory_space=pltpu.VMEM)],
        out_specs=(pl.BlockSpec(memory_space=pl.ANY), pl.BlockSpec(memory_space=pltpu.SMEM)),
        scratch_shapes=[
            pltpu.VMEM((4, 5, B, B), F32),
            pltpu.VMEM((4, 5, B, B), F32),
            pltpu.VMEM((wide, wide), BF16),
            pltpu.VMEM((wide, wide), BF16),
            pltpu.VMEM((wide, wide), BF16),
            pltpu.VMEM((wide, wide), BF16),
            pltpu.VMEM((wide, wide), F32),
            pltpu.VMEM((wide, wide), BF16),
            pltpu.VMEM((wide, wide), BF16),
            pltpu.VMEM((4, 2, B, B), F32),
            pltpu.VMEM((4, 2, B, B), F32),
            pltpu.VMEM((2, 5, B, B), F32),
            pltpu.VMEM((8, B), F32),
            pltpu.VMEM((8, B), F32),
            pltpu.VMEM((8, B), F32),
            pltpu.VMEM((2 * rows, 8, B), F32),
            dma((4,)), dma((4,)), dma((4,)), dma((2, 4)), dma((4, 2)), dma((2,)), dma((2,)), dma((2,)), dma((2,)),
            dma((3,)),
        ],
        compiler_params=pltpu.CompilerParams(collective_id=0, has_side_effects=True, vmem_limit_bytes=40 * 2**20),
        cost_estimate=pl.CostEstimate(flops=4 * 10**9, bytes_accessed=4 * 10**6, transcendentals=0),
    )(density, pattern)


def solution(mesh):
    placed = (P(("grp", "row"), None, "blk", None), P(("grp", "row"), None))
    return jax.shard_map(
        local,
        mesh=mesh,
        in_specs=placed,
        out_specs=(P(("grp", "row"), None, "blk", None), P("grp")),
        check_vma=False,
    )
```

time: 106 us -> 32.2 us (0.30)
  blocking collectives: 52.4 us -> 0 us
  Pallas kernels: 0 us -> 28.3 us
  matrix products: 20.4 us -> 0 us
  waiting for transfers between devices: 13.4 us -> 0 us
  starting transfers between devices: 11.9 us -> 0 us
  other arithmetic: 3.61 us -> 0 us
  between operations: 2.61 us -> 0.65 us
  local copies, waits for them, and re-layouts: 1.49 us -> 3.11 us
    psum x1 -> x0, blocking collectives: 36.8 us -> none  [step_total(): return lax.psum(partial_value, ('row', 'blk'))]
    pallas_call x0 -> x1, Pallas kernels: none -> 28.3 us  [local(): pl.pallas_call(functools.partial(kernel, rows), out_shape=(jax.ShapeDtype...]
    dot_general x76 -> x0, matrix products: 20.4 us -> none  [block_product(): jnp.einsum('nxy,nyz->nxz', left[:, W + term], right[W + term:W + term + r...]
    all_to_all x2 -> x0, blocking collectives: 15.6 us -> none  [the longest x1 10.2 us: local(): lax.all_to_all(whole_rows, 'blk', split_axis=2, concat_axis=0, tiled=True)]
    ppermute x4 -> x0, waiting for transfers between devices: 13.4 us -> none  [the longest x2 12.2 us: padded(): before = lax.ppermute(last, axis, up)]
    ppermute x4 -> x0, starting transfers between devices: 11.9 us -> none  [the longest x2 6.22 us: padded(): before = lax.ppermute(last, axis, up)]
    unnamed x2 -> x6, local copies, waits for them, and re-layouts: 0.01 us -> 3.11 us
    another operation x1 -> x0, other arithmetic: 1.78 us -> none  [local(): totals = jnp.stack(occupancy)]
  transfers between devices with their start and end apart: 4 -> 0, of which waited for: 3 -> 0; matrix products, arithmetic and copies ran while one was open for 3% -> 0% of each run, Pallas kernels for 0% -> 0%
where the time goes in v1:
time: 32.2 us; the launch traced here: 32 us
  Pallas kernels  28.3 us (88%)
  local copies, waits for them, and re-layouts  3.11 us (10%)
  between operations  0.65 us (2%)
    pallas_call x1, Pallas kernels, local(): pl.pallas_call(functools.partial(kernel, rows), out_shape=(jax.ShapeDtype...  28.3 us
    unnamed x6, local copies, waits for them, and re-layouts  3.11 us

profile of v1, /device:TPU:0, one launch (start us, length us, event | category | flops | bytes accessed | tf_op | source)
XLA Modules:
  0.0 32.0 jit_solution(343487857297510673)
XLA Ops:
  0.6 0.0 copy-start
  0.6 1.1 %copy-done = f32[4,5,64,128]{3,2,1,0:T(8,128)S(1)} copy-done((f32[4,5,64,128]{3,2,1,0:T(8,128)S(1)}, f32[4,5,64,128]{3,2,1,0:T(8,128)}, u32[]{:S(2)}) %copy-start) | copy-done | bytes 655384
  1.7 0.0 copy-start.1
  1.7 0.7 %copy-done.1 = s32[4,5]{1,0:T(4,128)S(1)} copy-done((s32[4,5]{1,0:T(4,128)S(1)}, s32[4,5]{1,0:T(4,128)}, u32[]{:S(2)}) %copy-start.1) | copy-done | bytes 104
  2.4 28.3 %shard_map.41 = (f32[4,5,64,128]{3,2,1,0:T(8,128)S(1)}, f32[2]{0:T(128)S(1)}) custom-call(f32[4,5,64,128]{3,2,1,0:T(8,128)S(1)} %copy-done, s32[4,5]{1,0:T(4,128)S(1)} %copy-done.1), custom_call_target="tpu_custom_call" | custom-call | flops 4000000000 | bytes 4000000 | tf_op jit(solution)/shard_map/pallas_call | solution.py:260
  30.7 0.8 %copy.6 = f32[4,5,64,128]{3,2,1,0:T(8,128)} copy(f32[4,5,64,128]{3,2,1,0:T(8,128)S(1)} %get-tuple-element.4) | data formatting | bytes 1310720
  31.5 0.5 %copy.7 = f32[2]{0:T(128)} copy(f32[2]{0:T(128)S(1)} %get-tuple-element.5) | data formatting | bytes 16
Async XLA Ops:
  0.6 1.1 %copy-start = (f32[4,5,64,128]{3,2,1,0:T(8,128)S(1)}, f32[4,5,64,128]{3,2,1,0:T(8,128)}, u32[]{:S(2)}) copy-start(f32[4,5,64,128]{3,2,1,0:T(8,128)} %dens.1) | copy-start | bytes 1966084
  1.7 0.7 %copy-start.1 = (s32[4,5]{1,0:T(4,128)S(1)}, s32[4,5]{1,0:T(4,128)}, u32[]{:S(2)}) copy-start(s32[4,5]{1,0:T(4,128)} %pat.1) | copy-start | bytes 244

commit v2 on v1

--- a/solution.py
+++ b/solution.py
@@ -13,6 +13,8 @@
 
 B = 128
 G, H, M, N = range(4)
+CHUNKS = ((0, 0, 2), (1, 0, 1), (3, 0, 1), (2, 0, 2), (1, 1, 2), (0, 2, 1))
+VMEM_BYTES = 40 * 2**20
 
 
 def span(first, last):
@@ -36,8 +38,9 @@
     return dot(lh[lat], rh[rat]) + dot(lh[lat], rl[rat]) + dot(ll[lat], rh[rat])
 
 
-def kernel(rows, dens, pat, out, occ, own, halo, dh, dl, sh, sl, s32, eh, el, xs, xr, res, patf, pathalo, tsend, trecv,
-           own_send, own_recv, own_loc, halo_send, halo_recv, pat_sem, x_send, x_recv, t_sem, out_sem):
+def kernel(rows, dens, pat, out, occ, own, halo, dh, dl, sh, sl, s32, eh, el, xs, xr, res, pati, patf, pathalo, tsend, trecv,
+           own_send, own_recv, own_loc, halo_send, halo_recv, relay_send,
+           relay_recv, pat_sem, x_send, x_recv, t_sem, out_sem):
     r, b = lax.axis_index("row"), lax.axis_index("blk")
     devices = 2 * rows
     me = 2 * r + b
@@ -58,13 +61,16 @@
         return carry
 
     lax.fori_loop(1, devices, greet, 0)
+    pat_in = pltpu.make_async_copy(pat, pati, pat_sem.at[2])
+    pat_in.start()
     local = []
     for i in range(4):
         copy = pltpu.make_async_copy(dens.at[i], own.at[i, :, half], own_loc.at[i])
         copy.start()
         local.append(copy)
     patf[...] = jnp.zeros_like(patf)
-    patf[0:4, 0:5] = pat[...].astype(F32)
+    pat_in.wait()
+    patf[0:4, 0:5] = pati[...].astype(F32)
     pl.semaphore_wait(barrier, devices - 1)
 
     sends = []
@@ -75,35 +81,58 @@
         sends.append(copy)
         return copy
 
-    def send_halo(d):
-        n = min(3, 4 - d)
-        send(dens.at[d, 2:2 + n], halo.at[d, 2:2 + n, half], halo_send.at[0, d], halo_recv.at[d, b],
-             {"row": after, "blk": 0})
-        send(dens.at[3 - d, 3 - n:3], halo.at[d, 3 - n:3, half], halo_send.at[1, d], halo_recv.at[d, b],
-             {"row": before, "blk": 1})
+    even = lax.rem(r, 2) == 0
+    toward = jnp.where(even, 1, -1)
+    direct = lax.rem(r + b, 2) == 1
+    relay_to = {"row": lax.rem(r + 4 * b - 2 + rows, rows), "blk": 1 - b}
+
+    def chunk_at(ref, side, c, *rest):
+        d, k, n = CHUNKS[c]
+        return ref.at[(d, pl.ds(jnp.where(side == 1, 2 + k, 3 - k - n), n)) + rest]
+
+    def send_halo(c):
+        d, k, n = CHUNKS[c]
+        i = jnp.where(even, d, 3 - d)
+        start = jnp.where(even, 2 + k, 3 - k - n)
+        send(dens.at[i, pl.ds(start, n)], chunk_at(halo, toward, c, half), halo_send.at[c], halo_recv.at[c, b],
+             {"row": lax.rem(r + toward + rows, rows), "blk": jnp.where(even, 0, 1)})
 
     pats = send(patf, pathalo, pat_sem.at[0], pat_sem.at[1], {"row": jnp.where(b == 0, after, before), "blk": b})
-    send_halo(3)
-    send_halo(2)
-    theirs = {}
+    for c in range(3):
+        send_halo(c)
     for q in range(4):
         i = 2 * (1 - b) + q if q < 2 else 2 * b + q - 2
         send(dens.at[i], own.at[i, :, half], own_send.at[q], own_recv.at[i], {"row": r, "blk": 1 - b})
-    send_halo(1)
-    send_halo(0)
+    for c in range(3, len(CHUNKS)):
+        send_halo(c)
 
     def wait_own(i):
         pltpu.make_async_copy(dens.at[i], own.at[i, :, half], own_loc.at[i]).wait()
         pltpu.make_async_remote_copy(dens.at[i], own.at[i, :, other_half], own_send.at[0], own_recv.at[i],
                                      device_id={"row": r, "blk": 1 - b}, device_id_type=MESH).wait_recv()
 
-    def wait_halo(d):
-        n = min(3, 4 - d)
-        start = jnp.where(b == 0, 2, 3 - n)
-        for c in range(2):
-            at = halo.at[d, pl.ds(start, n), 64 * c:64 * c + 64]
-            pltpu.make_async_remote_copy(at, at, halo_send.at[0, d], halo_recv.at[d, c],
-                                         device_id={"row": r, "blk": 1 - b}, device_id_type=MESH).wait_recv()
+    def relay(c):
+        at = chunk_at(halo, sign, c)
+        return pltpu.make_async_remote_copy(at, at, relay_send.at[c], relay_recv.at[c], device_id=relay_to,
+                                            device_id_type=MESH)
+
+    def wait_direct(*chunks):
+        @pl.when(direct)
+        def _():
+            for c in chunks:
+                for h in range(2):
+                    at = chunk_at(halo, sign, c, pl.ds(64 * h, 64))
+                    pltpu.make_async_remote_copy(at, at, halo_send.at[c], halo_recv.at[c, h], device_id=relay_to,
+                                                 device_id_type=MESH).wait_recv()
+                relay(c).start()
+
+    def wait_relayed(*chunks):
+        @pl.when(jnp.logical_not(direct))
+        def _():
+            for c in chunks:
+                at = chunk_at(halo, -sign, c)
+                pltpu.make_async_remote_copy(at, at, relay_send.at[c], relay_recv.at[c], device_id=relay_to,
+                                             device_id_type=MESH).wait_recv()
 
     def own_row(d):
         return jnp.where(b == 0, d - 4, 7 - d)
@@ -167,37 +196,43 @@
                 put(e, d, value.T)
     for d, e in ((2, 5), (5, 2), (4, 7), (7, 4)):
         clear(D, d, e)
+    wait_direct(0)
     square(D, M, M, H, N)
     square(D, M, N, M, N)
+    wait_direct(1)
     keep(M, N, M, N)
     xs[3, 0] = jnp.zeros((B, B), F32)
     other = {"row": r, "blk": 1 - b}
     send(xs.at[2:4], xr.at[2:4], x_send.at[0], x_recv.at[0], other)
 
-    def put_halo(d):
-        for k in range(min(3, 4 - d)):
-            value = halo[d, 2 + sign * k]
-            put(d, d + k, value)
-            if k:
-                put(d + k, d, value.T)
-
-    wait_halo(3)
-    put_halo(3)
-    wait_halo(2)
-    put_halo(2)
+    def put_halo(d, k):
+        value = halo[jnp.where(direct, d, 3 - d - k), 2 + sign * k * jnp.where(direct, 1, -1)]
+        if k == 0:
+            put(d, d, value)
+        else:
+            turned = value.T
+            put(d, d + k, jnp.where(direct, value, turned))
+            put(d + k, d, jnp.where(direct, turned, value))
+
+    wait_direct(2, 3)
+    wait_relayed(0, 1)
+    put_halo(3, 0)
+    put_halo(2, 0)
+    put_halo(2, 1)
     square(D, M, H, H, M)
     keep(M, M, H, N)
     send(xs.at[0:2], xr.at[0:2], x_send.at[1], x_recv.at[1], other)
     tsend[...] = jnp.zeros_like(tsend)
     tsend[0:1, :] = trace(xs[0, 0], xs[1, 1])
+    wait_direct(4)
     keep(M, H, H, M)
     pats.wait_recv()
     square(D, H, M, H, M)
 
-    wait_halo(1)
-    put_halo(1)
-    wait_halo(0)
-    put_halo(0)
+    wait_direct(5)
+    wait_relayed(2, 3, 4, 5)
+    for d, k in ((0, 0), (0, 1), (0, 2), (1, 0), (1, 1), (1, 2)):
+        put_halo(d, k)
     clear(D, 0, 3)
     clear(D, 3, 0)
     square(D, H, G, G, H)
@@ -247,6 +282,12 @@
     occ[0] = jnp.sum(total[0:1, :])
     occ[1] = jnp.sum(total[1:2, :])
     told.wait_send()
+
+    @pl.when(direct)
+    def _():
+        for c in range(len(CHUNKS)):
+            relay(c).wait_send()
+
     for copy in sends:
         copy.wait_send()
     mine.wait()
@@ -260,7 +301,7 @@
     return pl.pallas_call(
         functools.partial(kernel, rows),
         out_shape=(jax.ShapeDtypeStruct(density.shape, F32), jax.ShapeDtypeStruct((2,), F32)),
-        in_specs=[pl.BlockSpec(memory_space=pl.ANY), pl.BlockSpec(memory_space=pltpu.VMEM)],
+        in_specs=[pl.BlockSpec(memory_space=pltpu.HBM), pl.BlockSpec(memory_space=pltpu.HBM)],
         out_specs=(pl.BlockSpec(memory_space=pl.ANY), pl.BlockSpec(memory_space=pltpu.SMEM)),
         scratch_shapes=[
             pltpu.VMEM((4, 5, B, B), F32),
@@ -275,16 +316,17 @@
             pltpu.VMEM((4, 2, B, B), F32),
             pltpu.VMEM((4, 2, B, B), F32),
             pltpu.VMEM((2, 5, B, B), F32),
+            pltpu.VMEM((4, 5), jnp.int32),
             pltpu.VMEM((8, B), F32),
             pltpu.VMEM((8, B), F32),
             pltpu.VMEM((8, B), F32),
             pltpu.VMEM((2 * rows, 8, B), F32),
-            dma((4,)), dma((4,)), dma((4,)), dma((2, 4)), dma((4, 2)), dma((2,)), dma((2,)), dma((2,)), dma((2,)),
+            dma((4,)), dma((4,)), dma((4,)), dma((6,)), dma((6, 2)), dma((6,)), dma((6,)), dma((3,)), dma((2,)), dma((2,)), dma((2,)),
             dma((3,)),
         ],
-        compiler_params=pltpu.CompilerParams(collective_id=0, has_side_effects=True, vmem_limit_bytes=40 * 2**20),
+        compiler_params=pltpu.CompilerParams(collective_id=0, has_side_effects=True, vmem_limit_bytes=VMEM_BYTES),
         cost_estimate=pl.CostEstimate(flops=4 * 10**9, bytes_accessed=4 * 10**6, transcendentals=0),
-    )(density, pattern)
+    )(pltpu.with_memory_space_constraint(density, pltpu.HBM), pltpu.with_memory_space_constraint(pattern, pltpu.HBM))
 
 
 def solution(mesh):

time: 32.2 us -> 29.9 us (0.929)
  local copies, waits for them, and re-layouts: 3.11 us -> 1.35 us
  Pallas kernels: 28.3 us -> 27.8 us
    unnamed x6 -> x2, local copies, waits for them, and re-layouts: 3.11 us -> 1.35 us
    pallas_call x1, Pallas kernels: 28.3 us -> 27.8 us  [local(): pl.pallas_call(functools.partial(kernel, rows), out_shape=(jax.ShapeDtype...]
where the time goes in v2:
time: 29.9 us; the launch traced here: 29.8 us
  Pallas kernels  27.8 us (93%)
  local copies, waits for them, and re-layouts  1.35 us (5%)
  between operations  0.64 us (2%)
    pallas_call x1, Pallas kernels, local(): pl.pallas_call(functools.partial(kernel, rows), out_shape=(jax.ShapeDtype...  27.8 us
    unnamed x2, local copies, waits for them, and re-layouts  1.35 us

profile of v2, /device:TPU:0, one launch (start us, length us, event | category | flops | bytes accessed | tf_op | source)
XLA Modules:
  0.0 29.8 jit_solution(8140578051777262604)
XLA Ops:
  0.6 27.8 %shard_map.41 = (f32[4,5,64,128]{3,2,1,0:T(8,128)S(1)}, f32[2]{0:T(128)S(1)}) custom-call(f32[4,5,64,128]{3,2,1,0:T(8,128)} %dens.1, s32[4,5]{1,0:T(4,128)} %pat.1), custom_call_target="tpu_custom_call" | custom-call | flops 4000000000 | bytes 4000000 | tf_op jit(solution)/shard_map/pallas_call | solution.py:301
  28.4 0.8 %copy.6 = f32[4,5,64,128]{3,2,1,0:T(8,128)} copy(f32[4,5,64,128]{3,2,1,0:T(8,128)S(1)} %get-tuple-element.4) | data formatting | bytes 1310720
  29.3 0.5 %copy.7 = f32[2]{0:T(128)} copy(f32[2]{0:T(128)S(1)} %get-tuple-element.5) | data formatting | bytes 16

commit v3 on v2

--- a/solution.py
+++ b/solution.py
@@ -14,6 +14,7 @@
 B = 128
 G, H, M, N = range(4)
 CHUNKS = ((0, 0, 2), (1, 0, 1), (3, 0, 1), (2, 0, 2), (1, 1, 2), (0, 2, 1))
+RELAYED = 4
 VMEM_BYTES = 40 * 2**20
 
 
@@ -75,9 +76,13 @@
 
     sends = []
 
-    def send(src, dst, send_sem, recv_sem, device):
+    def start_copy(src, dst, send_sem, recv_sem, device):
         copy = pltpu.make_async_remote_copy(src, dst, send_sem, recv_sem, device_id=device, device_id_type=MESH)
         copy.start()
+        return copy
+
+    def send(*what):
+        copy = start_copy(*what)
         sends.append(copy)
         return copy
 
@@ -94,17 +99,25 @@
         d, k, n = CHUNKS[c]
         i = jnp.where(even, d, 3 - d)
         start = jnp.where(even, 2 + k, 3 - k - n)
-        send(dens.at[i, pl.ds(start, n)], chunk_at(halo, toward, c, half), halo_send.at[c], halo_recv.at[c, b],
-             {"row": lax.rem(r + toward + rows, rows), "blk": jnp.where(even, 0, 1)})
+        for q, step in enumerate((toward, -toward)[:1 if c < RELAYED else 2]):
+            start_copy(dens.at[i, pl.ds(start, n)], chunk_at(halo, toward, c, half), halo_send.at[q, c], halo_recv.at[c, b],
+                 {"row": lax.rem(r + step + rows, rows), "blk": jnp.where(step == 1, 0, 1)})
 
     pats = send(patf, pathalo, pat_sem.at[0], pat_sem.at[1], {"row": jnp.where(b == 0, after, before), "blk": b})
-    for c in range(3):
-        send_halo(c)
+    send_halo(0)
+    send_halo(1)
     for q in range(4):
         i = 2 * (1 - b) + q if q < 2 else 2 * b + q - 2
         send(dens.at[i], own.at[i, :, half], own_send.at[q], own_recv.at[i], {"row": r, "blk": 1 - b})
-    for c in range(3, len(CHUNKS)):
-        send_halo(c)
+
+    def second(c):
+        pltpu.make_async_remote_copy(chunk_at(halo, sign, c, half), chunk_at(halo, sign, c, half), halo_send.at[1, c],
+                                     halo_recv.at[c, b], device_id=relay_to, device_id_type=MESH).wait_send()
+
+    def sent(c):
+        pltpu.make_async_remote_copy(chunk_at(halo, sign, c, half), chunk_at(halo, sign, c, half), halo_send.at[0, c],
+                                     halo_recv.at[c, b], device_id=relay_to, device_id_type=MESH).wait_send()
+
 
     def wait_own(i):
         pltpu.make_async_copy(dens.at[i], own.at[i, :, half], own_loc.at[i]).wait()
@@ -116,23 +129,30 @@
         return pltpu.make_async_remote_copy(at, at, relay_send.at[c], relay_recv.at[c], device_id=relay_to,
                                             device_id_type=MESH)
 
+    def wait_halves(c, side):
+        for h in range(2):
+            at = chunk_at(halo, side, c, pl.ds(64 * h, 64))
+            pltpu.make_async_remote_copy(at, at, halo_send.at[0, c], halo_recv.at[c, h], device_id=relay_to,
+                                         device_id_type=MESH).wait_recv()
+
     def wait_direct(*chunks):
         @pl.when(direct)
         def _():
             for c in chunks:
-                for h in range(2):
-                    at = chunk_at(halo, sign, c, pl.ds(64 * h, 64))
-                    pltpu.make_async_remote_copy(at, at, halo_send.at[c], halo_recv.at[c, h], device_id=relay_to,
-                                                 device_id_type=MESH).wait_recv()
-                relay(c).start()
+                wait_halves(c, sign)
+                if c < RELAYED:
+                    relay(c).start()
 
     def wait_relayed(*chunks):
         @pl.when(jnp.logical_not(direct))
         def _():
             for c in chunks:
-                at = chunk_at(halo, -sign, c)
-                pltpu.make_async_remote_copy(at, at, relay_send.at[c], relay_recv.at[c], device_id=relay_to,
-                                             device_id_type=MESH).wait_recv()
+                if c < RELAYED:
+                    at = chunk_at(halo, -sign, c)
+                    pltpu.make_async_remote_copy(at, at, relay_send.at[c], relay_recv.at[c], device_id=relay_to,
+                                                 device_id_type=MESH).wait_recv()
+                else:
+                    wait_halves(c, -sign)
 
     def own_row(d):
         return jnp.where(b == 0, d - 4, 7 - d)
@@ -188,6 +208,8 @@
 
     for i in range(4):
         wait_own(i)
+    sent(0)
+    send_halo(2)
     for d in range(4, 8):
         for e in range(max(2, d - 2), min(8, d + 3)):
             value = own[own_row(d), 2 + sign * (e - d)]
@@ -197,9 +219,15 @@
     for d, e in ((2, 5), (5, 2), (4, 7), (7, 4)):
         clear(D, d, e)
     wait_direct(0)
+    sent(1)
+    send_halo(3)
     square(D, M, M, H, N)
+    sent(2)
+    send_halo(4)
+    wait_direct(1)
     square(D, M, N, M, N)
-    wait_direct(1)
+    sent(3)
+    send_halo(5)
     keep(M, N, M, N)
     xs[3, 0] = jnp.zeros((B, B), F32)
     other = {"row": r, "blk": 1 - b}
@@ -224,12 +252,11 @@
     send(xs.at[0:2], xr.at[0:2], x_send.at[1], x_recv.at[1], other)
     tsend[...] = jnp.zeros_like(tsend)
     tsend[0:1, :] = trace(xs[0, 0], xs[1, 1])
-    wait_direct(4)
     keep(M, H, H, M)
     pats.wait_recv()
     square(D, H, M, H, M)
 
-    wait_direct(5)
+    wait_direct(4, 5)
     wait_relayed(2, 3, 4, 5)
     for d, k in ((0, 0), (0, 1), (0, 2), (1, 0), (1, 1), (1, 2)):
         put_halo(d, k)
@@ -285,11 +312,14 @@
 
     @pl.when(direct)
     def _():
-        for c in range(len(CHUNKS)):
+        for c in range(RELAYED):
             relay(c).wait_send()
 
     for copy in sends:
         copy.wait_send()
+    for c in range(4, len(CHUNKS)):
+        sent(c)
+        second(c)
     mine.wait()
     yours.wait()
 
@@ -321,7 +351,7 @@
             pltpu.VMEM((8, B), F32),
             pltpu.VMEM((8, B), F32),
             pltpu.VMEM((2 * rows, 8, B), F32),
-            dma((4,)), dma((4,)), dma((4,)), dma((6,)), dma((6, 2)), dma((6,)), dma((6,)), dma((3,)), dma((2,)), dma((2,)), dma((2,)),
+            dma((4,)), dma((4,)), dma((4,)), dma((2, 6)), dma((6, 2)), dma((RELAYED,)), dma((RELAYED,)), dma((3,)), dma((2,)), dma((2,)), dma((2,)),
             dma((3,)),
         ],
         compiler_params=pltpu.CompilerParams(collective_id=0, has_side_effects=True, vmem_limit_bytes=VMEM_BYTES),

time: 29.9 us -> 29.3 us (0.980)
  Pallas kernels: 27.8 us -> 27.2 us
    pallas_call x1, Pallas kernels: 27.8 us -> 27.2 us  [local(): pl.pallas_call(functools.partial(kernel, rows), out_shape=(jax.ShapeDtype...]
where the time goes in v3:
time: 29.3 us; the launch traced here: 29.2 us
  Pallas kernels  27.2 us (93%)
  local copies, waits for them, and re-layouts  1.35 us (5%)
  between operations  0.64 us (2%)
    pallas_call x1, Pallas kernels, local(): pl.pallas_call(functools.partial(kernel, rows), out_shape=(jax.ShapeDtype...  27.2 us
    unnamed x2, local copies, waits for them, and re-layouts  1.35 us

profile of v3, /device:TPU:0, one launch (start us, length us, event | category | flops | bytes accessed | tf_op | source)
XLA Modules:
  0.0 29.2 jit_solution(3922317728795606436)
XLA Ops:
  0.6 27.2 %shard_map.41 = (f32[4,5,64,128]{3,2,1,0:T(8,128)S(1)}, f32[2]{0:T(128)S(1)}) custom-call(f32[4,5,64,128]{3,2,1,0:T(8,128)} %dens.1, s32[4,5]{1,0:T(4,128)} %pat.1), custom_call_target="tpu_custom_call" | custom-call | flops 4000000000 | bytes 4000000 | tf_op jit(solution)/shard_map/pallas_call | solution.py:331
  27.8 0.8 %copy.6 = f32[4,5,64,128]{3,2,1,0:T(8,128)} copy(f32[4,5,64,128]{3,2,1,0:T(8,128)S(1)} %get-tuple-element.4) | data formatting | bytes 1310720
  28.7 0.5 %copy.7 = f32[2]{0:T(128)} copy(f32[2]{0:T(128)S(1)} %get-tuple-element.5) | data formatting | bytes 16
